TPU v7x, 128 devices: a whole 4x4x4 slice. The times are simulated.
128 devices in a mesh: grp: 8 (over x, core), tp: 16 (over z, y).
Axes of the slice: x: 4, y: 4, z: 4, core: 2. Of those that a mesh axis runs over, the one named last changes fastest.
Arguments:
- activations: bfloat16 [4096, 8192], P('grp', 'tp'), may hold values from -6 to 6
- output_gradient: bfloat16 [4096, 8192], P('grp', 'tp'), may hold values from -6 to 6
- frozen_weight: bfloat16 [8192, 8192], P(None, 'tp'), may hold values from -0.0625 to 0.0625
- adapter_down_factors: bfloat16 [128, 32, 8192], P('grp', None, 'tp'), may hold values from -6 to 6
- adapter_up_factors: bfloat16 [128, 32, 8192], P('grp', None, 'tp'), may hold values from -6 to 6
- first_moment_down: float32 [128, 32, 8192], P('grp', None, 'tp'), may hold values from -6 to 6
- second_moment_down: float32 [128, 32, 8192], P('grp', None, 'tp'), may hold values from 0.5 to 2
- first_moment_up: float32 [128, 32, 8192], P('grp', None, 'tp'), may hold values from -6 to 6
- second_moment_up: float32 [128, 32, 8192], P('grp', None, 'tp'), may hold values from 0.5 to 2
- sample_row_prompt: int32 [8, 512], P('grp'), may hold values from 0 to 15, never falling along the last dimension, each value on 1 to 128 neighbouring positions
- majority_vote_reward: int32 [8, 512], P('grp'), may hold values 0 or 1
- prompt_adapter_slot: int32 [128], replicated, may hold values from 0 to 127, as said below
Outputs:
- layer_out: bfloat16 [4096, 8192], P('grp', 'tp')
- input_grad: bfloat16 [4096, 8192], P('grp', 'tp')
- updated_down_factors: bfloat16 [128, 32, 8192], P('grp', None, 'tp')
- updated_up_factors: bfloat16 [128, 32, 8192], P('grp', None, 'tp')
- updated_first_down: float32 [128, 32, 8192], P('grp', None, 'tp')
- updated_second_down: float32 [128, 32, 8192], P('grp', None, 'tp')
- updated_first_up: float32 [128, 32, 8192], P('grp', None, 'tp')
- updated_second_up: float32 [128, 32, 8192], P('grp', None, 'tp')
Inputs may be any that keep to these rules, and one draw needn't show every extreme that they name: `prompt_adapter_slot`: A permutation. Slots g * 16 to (g + 1) * 16 - 1 lie in group g's shard, and each group's shard holds the slots of exactly 2 prompts of every group.
All inputs are finite; a program needn't handle non-finite values. No bound on the sum of `majority_vote_reward` on one device may be relied on, other than what follows from the above.
Results may differ from a plain program's by a relative error of at most 0.0056.
Values may be sent and summed in bfloat16 or wider, within the bound.
No kernel may reach another device: no remote copies, remote signals or barrier semaphores. Data moves between devices by JAX's collectives and lax.ppermute only.
A program may use at most 192 MiB of HBM per device.

v0:
```python
import jax
import jax.numpy as jnp
from jax import lax
from jax.sharding import PartitionSpec as P

beta_first = 0.9
beta_second = 0.999
step_rate = 0.2
adam_eps = 1e-08
adapter_scale = 2.0


def moment_step_update(param, moment, second, grad):
    moment_new = beta_first * moment + (1.0 - beta_first) * grad
    second_new = beta_second * second + (1.0 - beta_second) * grad * grad
    param_new = param.astype(jnp.float32) - step_rate * moment_new / (
        jnp.sqrt(second_new) + adam_eps
    )
    return (param_new.astype(jnp.bfloat16), moment_new, second_new)


def local(
    activations,
    output_gradient,
    frozen_weight,
    adapter_down_factors,
    adapter_up_factors,
    first_moment_down,
    second_moment_down,
    first_moment_up,
    second_moment_up,
    sample_row_prompt,
    majority_vote_reward,
    prompt_adapter_slot,
):
    width = frozen_weight.shape[0]
    local_width = frozen_weight.shape[1]
    row_count = activations.shape[0]
    adapter_slot_count = adapter_down_factors.shape[0]
    adapter_rank_size = adapter_down_factors.shape[1]
    prompt_count = prompt_adapter_slot.shape[0]
    member = lax.axis_index("grp")
    scale_down = width ** (-0.5)
    scaled_up_factors = adapter_scale / adapter_rank_size**0.5
    contract_cols = (((1,), (1,)), ((), ()))
    contract_rows = (((0,), (0,)), ((), ()))
    labels = sample_row_prompt[0]
    onehot = (labels[:, None] == jnp.arange(adapter_slot_count, dtype=jnp.int32)[None, :]).astype(
        jnp.float32
    )
    reward = majority_vote_reward[0].astype(jnp.float32)
    counts = jnp.sum(onehot, axis=0)
    mean_reward = jnp.sum(onehot * reward[:, None], axis=0) / counts
    advantage = reward - jnp.sum(onehot * mean_reward[None, :], axis=1)
    weighted = (advantage[:, None] * output_gradient.astype(jnp.float32)).astype(jnp.bfloat16)
    my_slots = lax.dynamic_slice_in_dim(
        prompt_adapter_slot, member * adapter_slot_count, adapter_slot_count
    )
    every_down, every_up = (
        lax.all_gather(adapter_down_factors, "grp", axis=0, tiled=True),
        lax.all_gather(adapter_up_factors, "grp", axis=0, tiled=True),
    )
    down_local = jnp.take(every_down, my_slots, axis=0)
    up_local = jnp.take(every_up, my_slots, axis=0)
    flattened_down = down_local.reshape(adapter_slot_count * adapter_rank_size, local_width)
    flattened_up = up_local.reshape(adapter_slot_count * adapter_rank_size, local_width)
    low_all = lax.dot_general(
        activations, flattened_down, contract_cols, preferred_element_type=jnp.float32
    )
    low_part = jnp.sum(
        low_all.reshape(row_count, adapter_slot_count, adapter_rank_size) * onehot[:, :, None],
        axis=1,
    )
    back_all = lax.dot_general(
        weighted, flattened_up, contract_cols, preferred_element_type=jnp.float32
    )
    back_part = jnp.sum(
        back_all.reshape(row_count, adapter_slot_count, adapter_rank_size) * onehot[:, :, None],
        axis=1,
    )
    low_sum, back_sum = lax.psum((low_part, back_part), "tp")
    base_out = jnp.dot(
        lax.all_gather(activations, "tp", axis=1, tiled=True),
        frozen_weight,
        preferred_element_type=jnp.float32,
    )
    low = (scale_down * low_sum).astype(jnp.bfloat16)
    back_low = (scaled_up_factors * back_sum).astype(jnp.bfloat16)
    onehot_half = onehot.astype(jnp.bfloat16)
    low_wide = (onehot_half[:, :, None] * low[:, None, :]).reshape(
        row_count, adapter_slot_count * adapter_rank_size
    )
    back_wide = (onehot_half[:, :, None] * back_low[:, None, :]).reshape(
        row_count, adapter_slot_count * adapter_rank_size
    )
    layer_out = (
        base_out
        + scaled_up_factors * jnp.dot(low_wide, flattened_up, preferred_element_type=jnp.float32)
    ).astype(jnp.bfloat16)
    full_back = lax.dot_general(
        weighted, frozen_weight, contract_cols, preferred_element_type=jnp.float32
    )
    input_sum = lax.psum_scatter(full_back, "tp", scatter_dimension=1, tiled=True)
    input_grad = (
        input_sum
        + scale_down * jnp.dot(back_wide, flattened_down, preferred_element_type=jnp.float32)
    ).astype(jnp.bfloat16)
    grad_down = scale_down * lax.dot_general(
        back_wide, activations, contract_rows, preferred_element_type=jnp.float32
    )
    grad_up = scaled_up_factors * lax.dot_general(
        low_wide, weighted, contract_rows, preferred_element_type=jnp.float32
    )
    grad_down = grad_down.astype(jnp.bfloat16).reshape(
        adapter_slot_count, adapter_rank_size, local_width
    )
    grad_up = grad_up.astype(jnp.bfloat16).reshape(
        adapter_slot_count, adapter_rank_size, local_width
    )
    holder_down = (
        jnp.zeros((prompt_count, adapter_rank_size, local_width), jnp.bfloat16)
        .at[my_slots]
        .set(grad_down)
    )
    holder_up = (
        jnp.zeros((prompt_count, adapter_rank_size, local_width), jnp.bfloat16)
        .at[my_slots]
        .set(grad_up)
    )
    down_factor_slot, up_factor_slot = (
        lax.psum_scatter(holder_down, "grp", scatter_dimension=0, tiled=True).astype(jnp.float32),
        lax.psum_scatter(holder_up, "grp", scatter_dimension=0, tiled=True).astype(jnp.float32),
    )
    updated_down_factors, updated_first_down, updated_second_down = moment_step_update(
        adapter_down_factors, first_moment_down, second_moment_down, down_factor_slot
    )
    updated_up_factors, updated_first_up, updated_second_up = moment_step_update(
        adapter_up_factors, first_moment_up, second_moment_up, up_factor_slot
    )
    return (
        layer_out,
        input_grad,
        updated_down_factors,
        updated_up_factors,
        updated_first_down,
        updated_second_down,
        updated_first_up,
        updated_second_up,
    )


def solution(mesh):
    in_specs = (
        P("grp", "tp"),
        P("grp", "tp"),
        P(None, "tp"),
        P("grp", None, "tp"),
        P("grp", None, "tp"),
        P("grp", None, "tp"),
        P("grp", None, "tp"),
        P("grp", None, "tp"),
        P("grp", None, "tp"),
        P("grp", None),
        P("grp", None),
        P(),
    )
    out_specs = (
        P("grp", "tp"),
        P("grp", "tp"),
        P("grp", None, "tp"),
        P("grp", None, "tp"),
        P("grp", None, "tp"),
        P("grp", None, "tp"),
        P("grp", None, "tp"),
        P("grp", None, "tp"),
    )
    return jax.shard_map(local, mesh=mesh, in_specs=in_specs, out_specs=out_specs, check_vma=False)
```

profile of v0, /device:TPU:1, one launch (start us, length us, event | category | flops | bytes accessed | tf_op | source)
XLA Modules:
  0.0 447.7 jit_solution(7492767387817051464)
XLA Ops:
  7.2 0.0 copy-start
  7.2 0.0 all-gather.6.cloned.1.call-start
  7.2 0.7 all-gather.6.cloned.1.call-update
  7.9 0.0 all-gather.8.cloned.1.call-start
  8.0 0.7 all-gather.8.cloned.1.call-update
  8.7 0.0 all-reduce.3.cloned.1.call-start
  8.7 0.7 convert_element_type.76
  9.4 0.8 fusion.14
  10.2 0.8 select_reduce_fusion
  11.0 0.7 compare_and_fusion
  11.7 0.7 fusion.15
  12.4 33.0 %all-gather.6.cloned.1.call-done = bf16[128,32,512]{2,1,0:T(8,128)(2,1)} async-done(((bf16[16,32,512]{2,1,0:T(8,128)(2,1)}), bf16[128,32,512]{2,1,0:T(8,128)(2,1)}) %all-gather.6.cloned.1.call-update) | async-done | bytes 4194320 | tf_op jit(solution)/shard_map/all_gather | solution.py:60
  45.5 2.8 gather_fusion
  48.2 0.1 broadcast_select_fusion.1
  48.4 1.5 fusion.23
  49.9 0.8 multiply_reduce_fusion
  50.6 28.6 %all-gather.8.cloned.1.call-done = bf16[128,32,512]{2,1,0:T(8,128)(2,1)} async-done(((bf16[16,32,512]{2,1,0:T(8,128)(2,1)}), bf16[128,32,512]{2,1,0:T(8,128)(2,1)}) %all-gather.8.cloned.1.call-update) | async-done | bytes 4194320 | tf_op jit(solution)/shard_map/all_gather | solution.py:61
  79.3 2.8 gather_fusion.1
  82.0 2.3 fusion.7
  84.4 0.0 all-reduce.3.cloned.1.call-update
  84.4 0.0 all-gather.4.cloned.1.call-start
  84.4 0.5 all-gather.4.cloned.1.call-update
  85.0 0.0 reduce-scatter.6.cloned.1.call-start
  85.0 80.4 %all-reduce.3.cloned.1.call-done = (f32[512,32]{0,1:T(8,128)}, f32[512,32]{0,1:T(8,128)}) async-done(((f32[512,32]{0,1:T(8,128)}, f32[512,32]{0,1:T(8,128)}), (f32[512,32]{0,1:T(8,128)}, f32[512,32]{0,1:T(8,128)})) %all-reduce.3.cloned.1.call-update) | async-done | bytes 131088 | tf_op jit(solution)/shard_map/psum | solution.py:81
  165.4 0.8 multiply_convert_fusion.2
  166.2 0.8 multiply_convert_fusion.1
  167.0 0.1 broadcast_multiply_fusion.1
  167.1 0.4 fusion.4
  167.6 2.5 broadcast.85.clone
  170.1 2.6 scatter_fusion
  172.6 0.0 reduce-scatter.6.cloned.1.call-update
  172.6 0.0 reduce-scatter.8.cloned.1.call-start
  172.7 0.5 fusion.5
  173.2 2.5 broadcast.85.clone.1
  175.7 2.6 scatter_fusion.1
  178.3 0.0 reduce-scatter.8.cloned.1.call-update
  178.3 0.0 reduce-scatter.4.cloned.1.call-start
  178.4 11.8 %fusion.18 = f32[512,8192]{1,0:T(8,128)} fusion(bf16[8192,512]{1,0:T(8,128)(2,1)} %param.16, bf16[512,512]{1,0:T(8,128)(2,1)S(1)} %copy-done.4, f32[512]{0:T(512)S(1)} %sub.13), kind=kOutput, calls=%fused_computation.48 | convolution fusion | flops 4295753728 | bytes 25692160 | tf_op jit(solution)/shard_map/dot_general | solution.py:100
  190.1 0.0 reduce-scatter.4.cloned.1.call-update
  190.2 1.5 fusion.1
  191.7 54.1 %all-gather.4.cloned.1.call-done = bf16[512,8192]{1,0:T(8,128)(2,1)} async-done(((bf16[512,512]{1,0:T(8,128)(2,1)}), bf16[512,8192]{1,0:T(8,128)(2,1)}) %all-gather.4.cloned.1.call-update) | async-done | bytes 8388624 | tf_op jit(solution)/shard_map/all_gather | solution.py:83
  245.8 11.3 %fusion.6 = bf16[512,512]{1,0:T(8,128)(2,1)} fusion(f32[512,512]{1,0:T(8,128)} %fusion.1, bf16[512,8192]{1,0:T(8,128)(2,1)} %all-gather.4.cloned.1.call-done, bf16[8192,512]{1,0:T(8,128)(2,1)} %param.16), kind=kOutput, calls=%fused_computation.20 | convolution fusion | flops 4295491584 | bytes 18350080 | tf_op jit(solution)/shard_map/dot_general | solution.py:82
  257.1 26.1 %reduce-scatter.6.cloned.1.call-done = bf16[16,32,512]{2,1,0:T(8,128)(2,1)} async-done(((bf16[128,32,512]{2,1,0:T(8,128)(2,1)}), bf16[16,32,512]{2,1,0:T(8,128)(2,1)}) %reduce-scatter.6.cloned.1.call-update) | async-done | bytes 524304 | tf_op jit(solution)/shard_map/reduce_scatter | solution.py:131
  283.2 3.3 subtract_convert_fusion.1
  286.5 35.9 %reduce-scatter.8.cloned.1.call-done = bf16[16,32,512]{2,1,0:T(8,128)(2,1)} async-done(((bf16[128,32,512]{2,1,0:T(8,128)(2,1)}), bf16[16,32,512]{2,1,0:T(8,128)(2,1)}) %reduce-scatter.8.cloned.1.call-update) | async-done | bytes 524304 | tf_op jit(solution)/shard_map/reduce_scatter | solution.py:132
  322.4 3.6 subtract_convert_fusion
  326.1 112.3 %reduce-scatter.4.cloned.1.call-done = f32[512,512]{1,0:T(8,128)} async-done(((f32[512,8192]{1,0:T(8,128)}), f32[512,512]{1,0:T(8,128)}) %reduce-scatter.4.cloned.1.call-update) | async-done | bytes 1048592 | tf_op jit(solution)/shard_map/reduce_scatter | solution.py:103
  438.3 2.5 fusion.3
  (12 shorter events, 0.0 us)
Async XLA Ops:
  7.2 160.0 %copy-start = (bf16[512,512]{1,0:T(8,128)(2,1)S(1)}, bf16[512,512]{1,0:T(8,128)(2,1)}, u32[]{:S(2)}) copy-start(bf16[512,512]{1,0:T(8,128)(2,1)} %param.14) | copy-start | bytes 1572868
  7.2 38.3 %all-gather.6.cloned.1.call-start = ((), (), s32[]{:S(2)}) async-start(), calls=%async_computation.4 | async-start | bytes 4718592 | tf_op jit(solution)/shard_map/all_gather | solution.py:60
  7.9 71.3 %all-gather.8.cloned.1.call-start = ((), (), s32[]{:S(2)}) async-start(), calls=%async_computation.5 | async-start | bytes 4718592 | tf_op jit(solution)/shard_map/all_gather | solution.py:61
  8.7 156.7 %all-reduce.3.cloned.1.call-start = ((), (), s32[]{:S(2)}) async-start(), calls=%async_computation.9 | async-start | bytes 262144 | tf_op jit(solution)/shard_map/psum | solution.py:81
  82.0 90.7 %copy-start.4 = (bf16[512,512]{1,0:T(8,128)(2,1)S(1)}, bf16[512,512]{1,0:T(8,128)(2,1)}, u32[]{:S(2)}) copy-start(bf16[512,512]{1,0:T(8,128)(2,1)} %param.15) | copy-start | bytes 1572868
  84.4 161.4 %all-gather.4.cloned.1.call-start = ((), (), s32[]{:S(2)}) async-start(), calls=%async_computation.3 | async-start | bytes 8912896 | tf_op jit(solution)/shard_map/all_gather | solution.py:83
  85.0 198.2 %reduce-scatter.6.cloned.1.call-start = ((), (), s32[]{:S(2)}) async-start(), calls=%async_computation.7 | async-start | bytes 4718592 | tf_op jit(solution)/shard_map/reduce_scatter | solution.py:131
  172.6 149.8 %reduce-scatter.8.cloned.1.call-start = ((), (), s32[]{:S(2)}) async-start(), calls=%async_computation.8 | async-start | bytes 4718592 | tf_op jit(solution)/shard_map/reduce_scatter | solution.py:132
  178.3 260.0 %reduce-scatter.4.cloned.1.call-start = ((), (), s32[]{:S(2)}) async-start(), calls=%async_computation.6 | async-start | bytes 17825792 | tf_op jit(solution)/shard_map/reduce_scatter | solution.py:103
  191.7 91.5 %copy-start.1 = (bf16[16,32,512]{2,1,0:T(8,128)(2,1)S(1)}, bf16[16,32,512]{2,1,0:T(8,128)(2,1)}, u32[]{:S(2)}) copy-start(bf16[16,32,512]{2,1,0:T(8,128)(2,1)} %param.17) | copy-start | bytes 1572868
  191.7 91.5 %copy-start.3 = (f32[16,32,512]{2,1,0:T(8,128)S(1)}, f32[16,32,512]{2,1,0:T(8,128)}, u32[]{:S(2)}) copy-start(f32[16,32,512]{2,1,0:T(8,128)} %param.19) | copy-start | bytes 3145732
  191.7 130.8 %copy-start.2 = (bf16[16,32,512]{2,1,0:T(8,128)(2,1)S(1)}, bf16[16,32,512]{2,1,0:T(8,128)(2,1)}, u32[]{:S(2)}) copy-start(bf16[16,32,512]{2,1,0:T(8,128)(2,1)} %param.18) | copy-start | bytes 1572868
Sparse Core Ops, SparseCore 0:
  9.7 35.6 all-gather.5
  47.2 32.0 all-gather.7
  84.5 80.8 all-reduce.2
  167.5 78.2 all-gather.3
  248.2 34.9 reduce-scatter.5
  285.6 36.8 reduce-scatter.7
  326.2 112.0 reduce-scatter.3
where the time goes:
time: 448 us
  waiting for transfers between devices  372 us (83%)
  matrix products  31.8 us (7%)
  local copies, waits for them, and re-layouts  15.6 us (3%)
  between operations  14.2 us (3%)
  other arithmetic  13.3 us (3%)
    reduce_scatter x1, waiting for transfers between devices, local(): lax.psum_scatter(full_back, 'tp', scatter_dimension=1, tiled=True)  112 us
    psum x1, waiting for transfers between devices, local(): low_sum, back_sum = lax.psum((low_part, back_part), 'tp')  80.4 us
    all_gather x1, waiting for transfers between devices, local(): lax.all_gather(activations, 'tp', axis=1, tiled=True)  54.1 us
    reduce_scatter x1, waiting for transfers between devices, local(): lax.psum_scatter(holder_up, 'grp', scatter_dimension=0, tiled=True)  35.9 us
    all_gather x1, waiting for transfers between devices, local(): lax.all_gather(adapter_down_factors, 'grp', axis=0, tiled=True)  33 us
    all_gather x1, waiting for transfers between devices, local(): lax.all_gather(adapter_up_factors, 'grp', axis=0, tiled=True)  28.6 us
    reduce_scatter x1, waiting for transfers between devices, local(): lax.psum_scatter(holder_down, 'grp', scatter_dimension=0, tiled=True)  26.1 us
    dot_general x1, matrix products, local(): lax.dot_general(weighted, frozen_weight, contract_cols, preferred_element...  11.8 us
  transfers between devices with their start and end apart: 7, of which 7 were waited for; matrix products, arithmetic and copies ran while one was open for 12% of the time, Pallas kernels for 0%

commit v1 on v0

--- a/solution.py
+++ b/solution.py
@@ -80,7 +80,9 @@
     )
     low_sum, back_sum = lax.psum((low_part, back_part), "tp")
     base_out = jnp.dot(
-        lax.all_gather(activations, "tp", axis=1, tiled=True),
+        jnp.concatenate(
+            lax.all_to_all(jnp.stack([activations] * lax.axis_size("tp")), "tp", 0, 0), axis=1
+        ),
         frozen_weight,
         preferred_element_type=jnp.float32,
     )

time: 448 us -> 426 us (0.951)
  waiting for transfers between devices: 372 us -> 341 us
  starting transfers between devices: 0.28 us -> 5.17 us
    all_to_all x0 -> x1, waiting for transfers between devices: none -> 131 us  [local(): lax.all_to_all(jnp.stack([activations] * lax.axis_size('tp')), 'tp', 0, 0)]
    all_gather x1 -> x0, waiting for transfers between devices: 54.1 us -> none  [local(): lax.all_gather(activations, 'tp', axis=1, tiled=True)]
    reduce_scatter x1, waiting for transfers between devices: 112 us -> 66 us  [local(): lax.psum_scatter(full_back, 'tp', scatter_dimension=1, tiled=True)]
    reduce_scatter x1, waiting for transfers between devices: 35.9 us -> 0.01 us  [local(): lax.psum_scatter(holder_up, 'grp', scatter_dimension=0, tiled=True)]
    reduce_scatter x1, waiting for transfers between devices: 26.1 us -> 0.01 us  [local(): lax.psum_scatter(holder_down, 'grp', scatter_dimension=0, tiled=True)]
    all_to_all x0 -> x1, starting transfers between devices: none -> 4.94 us  [local(): lax.all_to_all(jnp.stack([activations] * lax.axis_size('tp')), 'tp', 0, 0)]
    another operation x2 -> x3, local copies, waits for them, and re-layouts: 4.94 us -> 9.07 us
  transfers between devices with their start and end apart: 7 -> 7, of which waited for: 7 -> 5; matrix products, arithmetic and copies ran while one was open for 12% -> 12% of each run, Pallas kernels for 0% -> 0%
where the time goes in v1:
time: 426 us
  waiting for transfers between devices  341 us (80%)
  matrix products  32.2 us (8%)
  local copies, waits for them, and re-layouts  20 us (5%)
  between operations  14.2 us (3%)
  other arithmetic  13.4 us (3%)
  starting transfers between devices  5.17 us (1%)
    all_to_all x1, waiting for transfers between devices, local(): lax.all_to_all(jnp.stack([activations] * lax.axis_size('tp')), 'tp', 0, 0)  131 us
    psum x1, waiting for transfers between devices, local(): low_sum, back_sum = lax.psum((low_part, back_part), 'tp')  80.9 us
    reduce_scatter x1, waiting for transfers between devices, local(): lax.psum_scatter(full_back, 'tp', scatter_dimension=1, tiled=True)  66 us
    all_gather x1, waiting for transfers between devices, local(): lax.all_gather(adapter_down_factors, 'grp', axis=0, tiled=True)  33 us
    all_gather x1, waiting for transfers between devices, local(): lax.all_gather(adapter_up_factors, 'grp', axis=0, tiled=True)  28.6 us
    dot_general x1, matrix products, local(): lax.dot_general(weighted, frozen_weight, contract_cols, preferred_element...  11.8 us
    dot_general x1, matrix products, local(): jnp.dot(jnp.concatenate(lax.all_to_all(jnp.stack([activations] * lax.axis...  11.7 us
  transfers between devices with their start and end apart: 7, of which 5 were waited for; matrix products, arithmetic and copies ran while one was open for 12% of the time, Pallas kernels for 0%

profile of v1, /device:TPU:1, one launch (start us, length us, event | category | flops | bytes accessed | tf_op | source)
XLA Modules:
  0.0 425.6 jit_solution(1518150475210743654)
XLA Ops:
  7.2 0.0 copy-start
  7.2 0.0 all-gather.3.cloned.1.call-start
  7.2 0.7 all-gather.3.cloned.1.call-update
  7.9 0.0 all-gather.5.cloned.1.call-start
  8.0 0.7 all-gather.5.cloned.1.call-update
  8.7 0.0 all-reduce.3.cloned.1.call-start
  8.7 0.7 convert_element_type.76
  9.4 0.8 fusion.14
  10.2 0.8 select_reduce_fusion
  11.0 0.7 compare_and_fusion
  11.7 0.7 fusion.15
  12.4 33.0 %all-gather.3.cloned.1.call-done = bf16[128,32,512]{2,1,0:T(8,128)(2,1)} async-done(((bf16[16,32,512]{2,1,0:T(8,128)(2,1)}), bf16[128,32,512]{2,1,0:T(8,128)(2,1)}) %all-gather.3.cloned.1.call-update) | async-done | bytes 4194320 | tf_op jit(solution)/shard_map/all_gather | solution.py:60
  45.5 2.8 gather_fusion
  48.2 0.1 broadcast_select_fusion.1
  48.4 1.5 fusion.23
  49.9 0.8 multiply_reduce_fusion
  50.6 28.6 %all-gather.5.cloned.1.call-done = bf16[128,32,512]{2,1,0:T(8,128)(2,1)} async-done(((bf16[16,32,512]{2,1,0:T(8,128)(2,1)}), bf16[128,32,512]{2,1,0:T(8,128)(2,1)}) %all-gather.5.cloned.1.call-update) | async-done | bytes 4194320 | tf_op jit(solution)/shard_map/all_gather | solution.py:61
  79.3 2.8 gather_fusion.1
  82.0 2.2 fusion.7
  84.3 0.0 all-reduce.3.cloned.1.call-update
  84.3 0.0 reduce-scatter.6.cloned.1.call-start
  84.4 80.9 %all-reduce.3.cloned.1.call-done = (f32[512,32]{0,1:T(8,128)}, f32[512,32]{0,1:T(8,128)}) async-done(((f32[512,32]{0,1:T(8,128)}, f32[512,32]{0,1:T(8,128)}), (f32[512,32]{0,1:T(8,128)}, f32[512,32]{0,1:T(8,128)})) %all-reduce.3.cloned.1.call-update) | async-done | bytes 131088 | tf_op jit(solution)/shard_map/psum | solution.py:81
  165.3 0.8 multiply_convert_fusion.2
  166.1 0.8 multiply_convert_fusion.1
  167.0 0.1 broadcast_multiply_fusion.1
  167.1 0.4 fusion.5
  167.5 2.6 broadcast.87.clone
  170.1 2.6 scatter_fusion
  172.7 0.0 reduce-scatter.6.cloned.1.call-update
  172.7 0.0 reduce-scatter.8.cloned.1.call-start
  172.8 0.0 copy-done.4
  172.8 0.5 fusion.6
  173.3 2.5 broadcast.87.clone.1
  175.8 2.6 scatter_fusion.1
  178.4 0.0 reduce-scatter.8.cloned.1.call-update
  178.4 0.0 reduce-scatter.4.cloned.1.call-start
  178.4 11.8 %fusion.18 = f32[512,8192]{1,0:T(8,128)} fusion(bf16[8192,512]{1,0:T(8,128)(2,1)} %param.16, bf16[512,512]{1,0:T(8,128)(2,1)S(1)} %copy-done.4, f32[512]{0:T(512)S(1)} %sub.13), kind=kOutput, calls=%fused_computation.48 | convolution fusion | flops 4295753728 | bytes 25692160 | tf_op jit(solution)/shard_map/dot_general | solution.py:102
  190.2 0.0 reduce-scatter.4.cloned.1.call-update
  190.2 0.2 copy.21
  190.5 4.0 stack.2
  194.5 4.9 %all-to-all-start = ((bf16[16,512,512]{1,2,0:T(8,128)(2,1)}), bf16[16,512,512]{1,2,0:T(8,128)(2,1)}, u32[]{:S(2)}, u32[]{:S(2)}) async-start(bf16[16,512,512]{1,2,0:T(8,128)(2,1)} %stack.2), calls=%async_computation | async-start | bytes 16777216 | tf_op jit(solution)/shard_map/all_to_all | solution.py:84
  199.4 1.5 fusion.1
  200.9 130.5 %all-to-all-done = bf16[16,512,512]{1,2,0:T(8,128)(2,1)} async-done(((bf16[16,512,512]{1,2,0:T(8,128)(2,1)}), bf16[16,512,512]{1,2,0:T(8,128)(2,1)}, u32[]{:S(2)}, u32[]{:S(2)}) %all-to-all-start) | async-done | bytes 8388640 | tf_op jit(solution)/shard_map/all_to_all | solution.py:84
  331.4 11.7 %fusion.3 = bf16[512,512]{1,0:T(8,128)(2,1)} fusion(f32[512,512]{1,0:T(8,128)} %fusion.1, bf16[512,8192]{0,1:T(8,128)(2,1)} %bitcast.1, bf16[8192,512]{1,0:T(8,128)(2,1)} %param.16), kind=kOutput, calls=%fused_computation.17 | convolution fusion | flops 4295491584 | bytes 18350080 | tf_op jit(solution)/shard_map/dot_general | solution.py:82
  343.2 3.3 subtract_convert_fusion.1
  346.5 3.7 subtract_convert_fusion
  350.3 66.0 %reduce-scatter.4.cloned.1.call-done = f32[512,512]{1,0:T(8,128)} async-done(((f32[512,8192]{1,0:T(8,128)}), f32[512,512]{1,0:T(8,128)}) %reduce-scatter.4.cloned.1.call-update) | async-done | bytes 1048592 | tf_op jit(solution)/shard_map/reduce_scatter | solution.py:105
  416.3 2.5 fusion.4
  (13 shorter events, 0.0 us)
Async XLA Ops:
  7.2 159.9 %copy-start = (bf16[512,512]{1,0:T(8,128)(2,1)S(1)}, bf16[512,512]{1,0:T(8,128)(2,1)}, u32[]{:S(2)}) copy-start(bf16[512,512]{1,0:T(8,128)(2,1)} %param.14) | copy-start | bytes 1572868
  7.2 38.3 %all-gather.3.cloned.1.call-start = ((), (), s32[]{:S(2)}) async-start(), calls=%async_computation.4 | async-start | bytes 4718592 | tf_op jit(solution)/shard_map/all_gather | solution.py:60
  7.9 71.3 %all-gather.5.cloned.1.call-start = ((), (), s32[]{:S(2)}) async-start(), calls=%async_computation.5 | async-start | bytes 4718592 | tf_op jit(solution)/shard_map/all_gather | solution.py:61
  8.7 156.6 %all-reduce.3.cloned.1.call-start = ((), (), s32[]{:S(2)}) async-start(), calls=%async_computation.9 | async-start | bytes 262144 | tf_op jit(solution)/shard_map/psum | solution.py:81
  50.6 122.1 %copy-start.4 = (bf16[512,512]{1,0:T(8,128)(2,1)S(1)}, bf16[512,512]{1,0:T(8,128)(2,1)}, u32[]{:S(2)}) copy-start(bf16[512,512]{1,0:T(8,128)(2,1)} %param.15) | copy-start | bytes 1572868
  84.3 258.9 %reduce-scatter.6.cloned.1.call-start = ((), (), s32[]{:S(2)}) async-start(), calls=%async_computation.7 | async-start | bytes 4718592 | tf_op jit(solution)/shard_map/reduce_scatter | solution.py:133
  172.7 173.8 %reduce-scatter.8.cloned.1.call-start = ((), (), s32[]{:S(2)}) async-start(), calls=%async_computation.8 | async-start | bytes 4718592 | tf_op jit(solution)/shard_map/reduce_scatter | solution.py:134
  178.4 237.9 %reduce-scatter.4.cloned.1.call-start = ((), (), s32[]{:S(2)}) async-start(), calls=%async_computation.6 | async-start | bytes 17825792 | tf_op jit(solution)/shard_map/reduce_scatter | solution.py:105
  194.5 137.0 %all-to-all-start = ((bf16[16,512,512]{1,2,0:T(8,128)(2,1)}), bf16[16,512,512]{1,2,0:T(8,128)(2,1)}, u32[]{:S(2)}, u32[]{:S(2)}) async-start(bf16[16,512,512]{1,2,0:T(8,128)(2,1)} %stack.2), calls=%async_computation | async-start | bytes 16777216 | tf_op jit(solution)/shard_map/all_to_all | solution.py:84
  331.4 11.8 %copy-start.1 = (bf16[16,32,512]{2,1,0:T(8,128)(2,1)S(1)}, bf16[16,32,512]{2,1,0:T(8,128)(2,1)}, u32[]{:S(2)}) copy-start(bf16[16,32,512]{2,1,0:T(8,128)(2,1)} %param.17) | copy-start | bytes 1572868
  331.4 11.8 %copy-start.3 = (f32[16,32,512]{2,1,0:T(8,128)S(1)}, f32[16,32,512]{2,1,0:T(8,128)}, u32[]{:S(2)}) copy-start(f32[16,32,512]{2,1,0:T(8,128)} %param.19) | copy-start | bytes 3145732
  331.4 15.1 %copy-start.2 = (bf16[16,32,512]{2,1,0:T(8,128)(2,1)S(1)}, bf16[16,32,512]{2,1,0:T(8,128)(2,1)}, u32[]{:S(2)}) copy-start(bf16[16,32,512]{2,1,0:T(8,128)(2,1)} %param.18) | copy-start | bytes 1572868
Sparse Core Ops, SparseCore 0:
  9.7 35.6 all-gather.2
  47.2 32.0 all-gather.4
  84.4 80.8 all-reduce.2
  172.8 35.4 reduce-scatter.5
  210.7 37.7 reduce-scatter.7
  252.1 164.1 reduce-scatter.3
